TPU v7x, 32 devices: a whole 2x2x4 slice. The times are simulated.
32 devices in a mesh: groups: 2 (over y), ctx: 4 (over z), head: 2 (over x), tp: 2 (over core).
Axes of the slice: x: 2, y: 2, z: 4, core: 2. Of those that a mesh axis runs over, the one named last changes fastest.
Arguments:
- queries: bfloat16 [32, 2048, 128], P(('head', 'tp'), ('groups', 'ctx')), parts along dimension 1, may hold values from -80 to 80
- stretch_keys: bfloat16 [8, 2048, 128], P(('head', 'tp'), ('groups', 'ctx')), parts along dimension 1, may hold values from -120 to 120
- stretch_values: bfloat16 [8, 2048, 128], P(('head', 'tp'), ('groups', 'ctx')), parts along dimension 1, may hold values from -6 to 6
- cache_keys: bfloat16 [8, 32768, 128], P(('head', 'tp'), ('groups', 'ctx')), parts along dimension 1, may hold values from -6 to 6
- cache_values: bfloat16 [8, 32768, 128], P(('head', 'tp'), ('groups', 'ctx')), parts along dimension 1, may hold values from -6 to 6
- block_picks: int32 [4, 8, 16], P('groups'), parts along dimension 0, may hold values from 0 to 31, as said below
- block_table: int32 [64], P('groups'), parts along dimension 0, may hold values from 0 to 31, as said below
Outputs:
- attended: bfloat16 [32, 2048, 128], P(('head', 'tp'), ('groups', 'ctx')), parts along dimension 1
There are 2 independent parts, one for each index of `groups`. A program takes and returns all parts, laid end to end along the dimension named above; each array names one. Nothing has to cross between parts.
Inputs may be any that keep to these rules, and one draw needn't show every extreme that they name: `block_picks`: for each query block and KV head the 16 picks are different logical blocks; exactly 4 of them have slots on each of 4 different indices of ctx, slot s lying on index s // 8. `block_table`: A permutation of the 32 physical slots.
All inputs are finite; a program needn't handle non-finite values.
Results may differ from a plain program's by a relative error of at most 0.0032.
Values may be sent and summed in bfloat16 or wider, within the bound.
A program may use at most 64 MiB of HBM per device.

v0:
```python
import jax
import jax.numpy as jnp
import numpy as np
from jax import lax
from jax.sharding import PartitionSpec as P

BLOCK = 512
TOPK = 16


def shifted(value, axis, by):
    count = lax.axis_size(axis)
    pairs = [(i, i + by) for i in range(count) if 0 <= i + by < count]
    return lax.ppermute(value, axis, pairs)


def as_sent(value):

    def short(part):
        return part.astype(jnp.bfloat16) if part.dtype == jnp.float32 else part

    return jax.tree.map(short, value)


def partner(value, axis, bit):
    mask = 2**bit
    pairs = [(source, source ^ mask) for source in range(lax.axis_size(axis))]
    return lax.ppermute(value, axis, pairs)


def lookup(lookup_table, indices):
    entries = jnp.arange(lookup_table.shape[0], dtype=jnp.int32)
    return jnp.sum(jnp.where(indices[..., None] == entries, lookup_table, 0), axis=-1)


def owner_rank(owners):
    ordinal = jnp.arange(owners.shape[-1], dtype=jnp.int32)
    before = (owners[..., :, None] == owners[..., None, :]) & (ordinal[None, :] < ordinal[:, None])
    return jnp.sum(before, axis=-1)


def pick_rows(source, indices):
    return source[indices]


def take_blocks(blocks, indices):
    return jax.vmap(pick_rows)(blocks, indices)


def attend(query_rows, all_keys, all_values, allowed_mask):
    tile_relevance = jnp.einsum(
        "rd,kd->rk", query_rows, all_keys, preferred_element_type=jnp.float32
    )
    tile_relevance = tile_relevance * query_rows.shape[-1] ** (-0.5)
    tile_relevance = jnp.where(allowed_mask, tile_relevance, -jnp.inf)
    row_max = jnp.max(tile_relevance, axis=-1, keepdims=True)
    weights = jnp.exp(tile_relevance - row_max)
    weight_sum = jnp.sum(weights, axis=-1, keepdims=True)
    mixed = jnp.einsum(
        "rk,kd->rd", weights.astype(jnp.bfloat16), all_values, preferred_element_type=jnp.float32
    )
    return (mixed / weight_sum).astype(jnp.bfloat16)


def shards(
    queries, stretch_keys, stretch_values, cache_keys, cache_values, block_picks, block_table
):
    kv_dev, tok_dev, head_dim = stretch_keys.shape
    q_per_kv = queries.shape[0] // kv_dev
    blocks_dev = cache_keys.shape[1] // BLOCK
    ctx_size = lax.axis_size("ctx")
    ctx_index = lax.axis_index("ctx")
    per_peer = max(1, TOPK // ctx_size)
    parity = ctx_index % 2
    head_ids = lax.axis_index(("head", "tp")) * kv_dev + jnp.arange(kv_dev, dtype=jnp.int32)
    selector = head_ids[:, None] == jnp.arange(block_picks.shape[1], dtype=jnp.int32)[None, :]
    my_picks = jnp.sum(jnp.where(selector[None, :, :, None], block_picks[:, None, :, :], 0), axis=2)
    physical = lookup(block_table, my_picks)
    owners = physical // blocks_dev
    in_owner = physical % blocks_dev
    peer_rank = owner_rank(owners)
    targets = np.arange(ctx_size) * tok_dev // BLOCK
    target_owner = owners[targets]
    target_rank = peer_rank[targets]
    target_local = in_owner[targets]
    slot_ids = jnp.arange(per_peer, dtype=jnp.int32)
    matched = (target_owner[:, :, None, :] == ctx_index) & (
        target_rank[:, :, None, :] == slot_ids[None, None, :, None]
    )
    chosen = jnp.sum(jnp.where(matched, target_local[:, :, None, :], 0), axis=-1)
    usable = jnp.any(matched, axis=-1)
    chosen = jnp.transpose(chosen, (1, 0, 2)).reshape(kv_dev, ctx_size * per_peer)
    usable = jnp.transpose(usable, (1, 0, 2)).reshape(kv_dev, ctx_size * per_peer)
    my_block = ctx_index * tok_dev // BLOCK
    my_owner = lax.dynamic_index_in_dim(owners, my_block, 0, keepdims=False)
    my_rank = lax.dynamic_index_in_dim(peer_rank, my_block, 0, keepdims=False)
    my_slot = my_owner * per_peer + my_rank
    prev_keys, prev_values = shifted((stretch_keys, stretch_values), "ctx", 1)
    half_rows = BLOCK // 2
    key_halves = cache_keys.reshape(kv_dev, blocks_dev * 2, half_rows, head_dim)
    value_halves = cache_values.reshape(kv_dev, blocks_dev * 2, half_rows, head_dim)
    row_side = jnp.asarray(np.repeat(np.arange(ctx_size) % 2, per_peer), jnp.int32)
    half_index = chosen * 2 + row_side[None, :]
    sent_keys = jnp.where(usable[:, :, None, None], take_blocks(key_halves, half_index), 0).astype(
        jnp.bfloat16
    )
    sent_values = jnp.where(
        usable[:, :, None, None], take_blocks(value_halves, half_index), 0
    ).astype(jnp.bfloat16)
    got_keys, got_values = (
        lax.all_to_all(sent_keys, "ctx", split_axis=1, concat_axis=1, tiled=True),
        lax.all_to_all(sent_values, "ctx", split_axis=1, concat_axis=1, tiled=True),
    )
    mine_keys = take_blocks(got_keys, my_slot)
    mine_values = take_blocks(got_values, my_slot)
    other_keys, other_values = (
        partner(as_sent(mine_keys), "ctx", 0).astype(mine_keys.dtype),
        partner(as_sent(mine_values), "ctx", 0).astype(mine_values.dtype),
    )
    first_keys = jnp.where(parity == 0, mine_keys, other_keys)
    second_keys = jnp.where(parity == 0, other_keys, mine_keys)
    first_values = jnp.where(parity == 0, mine_values, other_values)
    second_values = jnp.where(parity == 0, other_values, mine_values)
    live_keys = jnp.concatenate([first_keys, second_keys], axis=2)
    live_values = jnp.concatenate([first_values, second_values], axis=2)
    span_cols = TOPK * BLOCK
    live_keys = live_keys.reshape(kv_dev, span_cols, head_dim)
    live_values = live_values.reshape(kv_dev, span_cols, head_dim)
    all_keys = jnp.concatenate([live_keys, prev_keys, stretch_keys], axis=1)
    all_values = jnp.concatenate([live_values, prev_values, stretch_values], axis=1)
    query_rows = queries.reshape(kv_dev, q_per_kv * tok_dev, head_dim)
    step_rows = min(512, q_per_kv * tok_dev)
    columns = jnp.arange(span_cols + 2 * tok_dev, dtype=jnp.int32)

    def one_head(packed):
        q_head, k_head, v_head = packed
        q_steps = q_head.reshape(-1, step_rows, head_dim)
        starts = jnp.arange(q_steps.shape[0], dtype=jnp.int32) * step_rows

        def one_step(packed_block_step):
            q_block, first_row = packed_block_step
            position = (first_row + jnp.arange(step_rows, dtype=jnp.int32)) % tok_dev
            cache_part = columns[None, :] < span_cols
            earlier_part = (
                (columns[None, :] >= span_cols)
                & (columns[None, :] < span_cols + tok_dev)
                & (columns[None, :] - span_cols > position[:, None])
                & (ctx_index > 0)
            )
            own_part = (columns[None, :] >= span_cols + tok_dev) & (
                columns[None, :] - span_cols - tok_dev <= position[:, None]
            )
            return attend(q_block, k_head, v_head, cache_part | earlier_part | own_part)

        return lax.map(one_step, (q_steps, starts)).reshape(q_per_kv * tok_dev, head_dim)

    result = lax.map(one_head, (query_rows, all_keys, all_values))
    return result.reshape(kv_dev * q_per_kv, tok_dev, head_dim)


def solution(mesh):
    placed = (
        P(("head", "tp"), ("groups", "ctx"), None),
        P(("head", "tp"), ("groups", "ctx"), None),
        P(("head", "tp"), ("groups", "ctx"), None),
        P(("head", "tp"), ("groups", "ctx"), None),
        P(("head", "tp"), ("groups", "ctx"), None),
        P("groups", None, None),
        P("groups"),
    )
    return jax.shard_map(
        shards,
        mesh=mesh,
        in_specs=placed,
        out_specs=P(("head", "tp"), ("groups", "ctx"), None),
        check_vma=False,
    )
```

profile of v0, /device:TPU:0, one launch (start us, length us, event | category | flops | bytes accessed | tf_op | source)
XLA Modules:
  0.0 363.7 jit_solution(13856905821156815247)
XLA Ops:
  0.1 0.9 select_reduce_fusion.2
  1.0 0.9 select_reduce_fusion
  1.9 0.7 pad_clamp_fusion
  5.1 0.7 fusion.27
  5.8 2.1 gather_fusion.3
  7.9 3.9 %gather_fusion.5 = bf16[32,256,128]{2,1,0:T(8,128)(2,1)} fusion(bf16[2,16,256,128]{3,2,1,0:T(8,128)(2,1)} %bitcast.67, s32[32]{0:T(128)S(1)} %reshape.259), kind=kCustom, calls=%fused_computation.5 | custom fusion | bytes 4194560 | tf_op jit(solution)/shard_map/vmap()/gather | solution.py:43
  11.9 3.2 broadcast_select_fusion
  15.2 1.6 copy.18
  16.7 6.3 %all-to-all-start = ((bf16[2,16,256,128]{3,2,0,1:T(8,128)(2,1)}), bf16[2,16,256,128]{3,2,0,1:T(8,128)(2,1)S(1)}, u32[]{:S(2)}, u32[]{:S(2)}) async-start(bf16[2,16,256,128]{3,2,0,1:T(8,128)(2,1)} %copy.18), calls=%async_computation | async-start | bytes 4194304 | tf_op jit(solution)/shard_map/all_to_all | solution.py:111
  23.1 3.1 copy.19
  26.2 45.1 %all-to-all-done = bf16[2,16,256,128]{3,2,0,1:T(8,128)(2,1)S(1)} async-done(((bf16[2,16,256,128]{3,2,0,1:T(8,128)(2,1)}), bf16[2,16,256,128]{3,2,0,1:T(8,128)(2,1)S(1)}, u32[]{:S(2)}, u32[]{:S(2)}) %all-to-all-start) | async-done | bytes 2097184 | tf_op jit(solution)/shard_map/all_to_all | solution.py:111
  71.3 4.5 %all-to-all-start.1 = ((bf16[2,16,256,128]{3,2,0,1:T(8,128)(2,1)}), bf16[2,16,256,128]{3,2,0,1:T(8,128)(2,1)}, u32[]{:S(2)}, u32[]{:S(2)}) async-start(bf16[2,16,256,128]{3,2,0,1:T(8,128)(2,1)} %copy.19), calls=%async_computation.1 | async-start | bytes 4194304 | tf_op jit(solution)/shard_map/all_to_all | solution.py:112
  75.9 2.6 gather_fusion.4
  78.5 2.0 collective-permute-start
  80.5 43.1 %all-to-all-done.1 = bf16[2,16,256,128]{3,2,0,1:T(8,128)(2,1)} async-done(((bf16[2,16,256,128]{3,2,0,1:T(8,128)(2,1)}), bf16[2,16,256,128]{3,2,0,1:T(8,128)(2,1)}, u32[]{:S(2)}, u32[]{:S(2)}) %all-to-all-start.1) | async-done | bytes 2097184 | tf_op jit(solution)/shard_map/all_to_all | solution.py:112
  123.6 3.7 %gather_fusion.6 = bf16[32,256,128]{2,1,0:T(8,128)(2,1)} fusion(bf16[2,16,256,128]{3,2,0,1:T(8,128)(2,1)} %all-to-all-done.1, s32[32]{0:T(128)S(1)} %reshape.265), kind=kCustom, calls=%fused_computation.6 | custom fusion | bytes 4194560 | tf_op jit(solution)/shard_map/vmap()/gather | solution.py:43
  127.3 3.9 %collective-permute-start.3 = (bf16[2,256,128]{2,1,0:T(8,128)(2,1)S(1)}, bf16[2,256,128]{2,1,0:T(8,128)(2,1)S(1)}, u32[]{:S(2)}, u32[]{:S(2)}) collective-permute-start(bf16[2,256,128]{2,1,0:T(8,128)(2,1)S(1)} %copy-done.5), channel_id=1, source_target_pairs={{0,4},{4,8},{8,12},{1,5},{5,9},{9,13},{2,6},{6,10},{10,14},{3,7},{... | collective-permute-start | bytes 393224 | tf_op jit(solution)/shard_map/ppermute | solution.py:14
  131.3 2.6 collective-permute-start.1
  134.0 24.3 %collective-permute-done = bf16[2,16,256,128]{3,2,1,0:T(8,128)(2,1)} collective-permute-done((bf16[2,16,256,128]{3,2,1,0:T(8,128)(2,1)S(1)}, bf16[2,16,256,128]{3,2,1,0:T(8,128)(2,1)}, u32[]{:S(2)}, u32[]{:S(2)}) %collective-permute-start) | collective-permute-done | bytes 2097184 | tf_op jit(solution)/shard_map/ppermute | solution.py:28
  158.3 43.0 %collective-permute-done.2 = bf16[2,16,256,128]{3,2,1,0:T(8,128)(2,1)} collective-permute-done((bf16[2,16,256,128]{3,2,1,0:T(8,128)(2,1)}, bf16[2,16,256,128]{3,2,1,0:T(8,128)(2,1)}, u32[]{:S(2)}, u32[]{:S(2)}) %collective-permute-start.2) | collective-permute-done | bytes 2097184 | tf_op jit(solution)/shard_map/ppermute | solution.py:28
  201.2 3.1 broadcast_select_fusion.3
  204.8 10.0 %pad_maximum_fusion.1 = bf16[2,8704,128]{2,1,0:T(8,128)(2,1)} fusion(bf16[2,256,128]{2,1,0:T(8,128)(2,1)S(1)} %copy-done.5, bf16[2,256,128]{2,1,0:T(8,128)(2,1)S(1)} %collective-permute-done.3, bf16[2,8192,128]{2,1,0:T(8,128)(2,1)S(1)} %bitcast.56), kind=kLoop, calls=%fused_computation.36 | loop fusion | flops 13369344 | bytes 8912896 | tf_op jit(solution)/shard_map/concatenate | solution.py:130
  215.2 9.9 %pad_maximum_fusion = bf16[2,8704,128]{2,1,0:T(8,128)(2,1)} fusion(bf16[2,256,128]{2,1,0:T(8,128)(2,1)S(1)} %copy-done.6, bf16[2,256,128]{2,1,0:T(8,128)(2,1)S(1)} %collective-permute-done.1, bf16[2,8192,128]{2,1,0:T(8,128)(2,1)S(1)} %bitcast.57), kind=kLoop, calls=%fused_computation.35 | loop fusion | flops 13369344 | bytes 8912896 | tf_op jit(solution)/shard_map/concatenate | solution.py:129
  225.1 136.7 %while.49 = (s32[]{:T(128)}, bf16[2,1024,128]{2,1,0:T(8,128)(2,1)S(1)}, bf16[2,1024,128]{2,1,0:T(8,128)(2,1)S(1)}, bf16[2,8704,128]{2,1,0:T(8,128)(2,1)}, bf16[2...) while((s32[]{:T(128)}, ...), condition=%wide.region_10.11_spmd.clone.clone, body=%wide.region_5.10_spmd.clone.clone.sunk | while | flops 2344288768 | bytes 68473648 | solution.py:157
  225.1 3.9 %dynamic-slice_bitcast_fusion.3 = (bf16[8704,128]{1,0:T(8,128)(2,1)}, bf16[8704,128]{1,0:T(8,128)(2,1)}) fusion(bf16[2,8704,128]{2,1,0:T(8,128)(2,1)} %get-tuple-element.681, s32[]{:T(128)} %get-tuple-element.668, bf16[2,8704,128]{2,1,0:T(8,128)(2,1)} %get-tuple-element.680), kind=kLoop, calls=%fused_computation.30.clone.1 | loop fusion | bytes 8912900 | tf_op jit(solution)/shard_map/while/body/jit(dynamic_index_in_dim)/squeeze | solution.py:157
  229.1 64.4 %while.50 = (s32[]{:T(128)}, bf16[2,512,128]{2,1,0:T(8,128)(2,1)S(1)}, s32[8704]{0:T(1024)S(1)}, s32[2]{0:T(128)S(1)}, pred[]{:T(512)}, /*index=5*/bf16[2,512,12...) while((s32[]{:T(128)}, ...), condition=%wide.region_9.9_spmd.clone, body=%wide.region_6.8_spmd.clone.sunk | while | flops 2344288768 | bytes 58477172 | solution.py:155
  229.1 0.6 dynamic_slice.85
  229.7 0.6 add_select_fusion.2
  230.4 13.1 %fusion.43 = (f32[512]{0:T(512)S(1)}, f32[512,8704]{1,0:T(8,128)}) fusion(bf16[8704,128]{1,0:T(8,128)(2,1)} %get-tuple-element.656, bf16[2,512,128]{2,1,0:T(8,128)(2,1)S(1)} %get-tuple-element.655, s32[]{:T(128)} %get-tuple-element.641, s32[8704]{0:T(1024)S(1)} %get-tuple-element.625, pred[8704]{0:T(1024)(128)(4,1)S(1)} %get-tuple-element.626, ...), kind=kOutput, calls=%fused_computation.75.clone.1 | convolution fusion | flops 1185414656 | bytes 20290564 | tf_op jit(solution)/shard_map/while/body/eval_jaxpr/while/body/eval_jaxpr/rd,kd->rk/dot_general | solution.py:51
  243.4 8.5 %fusion.44 = f32[512]{0:T(512)S(1)} fusion(f32[512,8704]{1,0:T(8,128)} %get-tuple-element.630, f32[512]{0:T(512)S(1)} %get-tuple-element.631), kind=kLoop, calls=%fused_computation.10.clone.1 | loop fusion | flops 8912384 | bytes 17829888 | tf_op jit(solution)/shard_map/while/body/eval_jaxpr/while/body/eval_jaxpr/reduce_sum | solution.py:58
  252.0 9.3 %fusion.45 = bf16[2,512,128]{2,1,0:T(8,128)(2,1)S(1)} fusion(bf16[2,512,128]{2,1,0:T(8,128)(2,1)S(1)} %get-tuple-element.642, s32[]{:T(128)} %get-tuple-element.641, bf16[8704,128]{1,0:T(8,128)(2,1)} %get-tuple-element.657, f32[512,8704]{1,0:T(8,128)} %get-tuple-element.630, f32[512]{0:T(512)S(1)} %get-tuple-element.631, f32[512]{0:T(512)S(1)} %fusion.44), kind=kOutput, calls=%fused_computation.17.clone.1 | convolution fusion | flops 1149894656 | bytes 20189188 | tf_op jit(solution)/shard_map/while/body/eval_jaxpr/while/body/eval_jaxpr/rk,kd->rd/dot_general | solution.py:59
  261.3 0.6 dynamic_slice.85
  261.9 0.6 add_select_fusion.2
  262.5 13.1 %fusion.43 = (f32[512]{0:T(512)S(1)}, f32[512,8704]{1,0:T(8,128)}) fusion(bf16[8704,128]{1,0:T(8,128)(2,1)} %get-tuple-element.656, bf16[2,512,128]{2,1,0:T(8,128)(2,1)S(1)} %get-tuple-element.655, s32[]{:T(128)} %get-tuple-element.641, s32[8704]{0:T(1024)S(1)} %get-tuple-element.625, pred[8704]{0:T(1024)(128)(4,1)S(1)} %get-tuple-element.626, ...), kind=kOutput, calls=%fused_computation.75.clone.1 | convolution fusion | flops 1185414656 | bytes 20290564 | tf_op jit(solution)/shard_map/while/body/eval_jaxpr/while/body/eval_jaxpr/rd,kd->rk/dot_general | solution.py:51
  275.6 8.5 %fusion.44 = f32[512]{0:T(512)S(1)} fusion(f32[512,8704]{1,0:T(8,128)} %get-tuple-element.630, f32[512]{0:T(512)S(1)} %get-tuple-element.631), kind=kLoop, calls=%fused_computation.10.clone.1 | loop fusion | flops 8912384 | bytes 17829888 | tf_op jit(solution)/shard_map/while/body/eval_jaxpr/while/body/eval_jaxpr/reduce_sum | solution.py:58
  284.2 9.3 %fusion.45 = bf16[2,512,128]{2,1,0:T(8,128)(2,1)S(1)} fusion(bf16[2,512,128]{2,1,0:T(8,128)(2,1)S(1)} %get-tuple-element.642, s32[]{:T(128)} %get-tuple-element.641, bf16[8704,128]{1,0:T(8,128)(2,1)} %get-tuple-element.657, f32[512,8704]{1,0:T(8,128)} %get-tuple-element.630, f32[512]{0:T(512)S(1)} %get-tuple-element.631, f32[512]{0:T(512)S(1)} %fusion.44), kind=kOutput, calls=%fused_computation.17.clone.1 | convolution fusion | flops 1149894656 | bytes 20189188 | tf_op jit(solution)/shard_map/while/body/eval_jaxpr/while/body/eval_jaxpr/rk,kd->rd/dot_general | solution.py:59
  293.5 3.9 %dynamic-slice_bitcast_fusion.3 = (bf16[8704,128]{1,0:T(8,128)(2,1)}, bf16[8704,128]{1,0:T(8,128)(2,1)}) fusion(bf16[2,8704,128]{2,1,0:T(8,128)(2,1)} %get-tuple-element.681, s32[]{:T(128)} %get-tuple-element.668, bf16[2,8704,128]{2,1,0:T(8,128)(2,1)} %get-tuple-element.680), kind=kLoop, calls=%fused_computation.30.clone.1 | loop fusion | bytes 8912900 | tf_op jit(solution)/shard_map/while/body/jit(dynamic_index_in_dim)/squeeze | solution.py:157
  297.5 64.4 %while.50 = (s32[]{:T(128)}, bf16[2,512,128]{2,1,0:T(8,128)(2,1)S(1)}, s32[8704]{0:T(1024)S(1)}, s32[2]{0:T(128)S(1)}, pred[]{:T(512)}, /*index=5*/bf16[2,512,12...) while((s32[]{:T(128)}, ...), condition=%wide.region_9.9_spmd.clone, body=%wide.region_6.8_spmd.clone.sunk | while | flops 2344288768 | bytes 58477172 | solution.py:155
  298.1 0.6 add_select_fusion.2
  298.7 13.1 %fusion.43 = (f32[512]{0:T(512)S(1)}, f32[512,8704]{1,0:T(8,128)}) fusion(bf16[8704,128]{1,0:T(8,128)(2,1)} %get-tuple-element.656, bf16[2,512,128]{2,1,0:T(8,128)(2,1)S(1)} %get-tuple-element.655, s32[]{:T(128)} %get-tuple-element.641, s32[8704]{0:T(1024)S(1)} %get-tuple-element.625, pred[8704]{0:T(1024)(128)(4,1)S(1)} %get-tuple-element.626, ...), kind=kOutput, calls=%fused_computation.75.clone.1 | convolution fusion | flops 1185414656 | bytes 20290564 | tf_op jit(solution)/shard_map/while/body/eval_jaxpr/while/body/eval_jaxpr/rd,kd->rk/dot_general | solution.py:51
  311.8 8.5 %fusion.44 = f32[512]{0:T(512)S(1)} fusion(f32[512,8704]{1,0:T(8,128)} %get-tuple-element.630, f32[512]{0:T(512)S(1)} %get-tuple-element.631), kind=kLoop, calls=%fused_computation.10.clone.1 | loop fusion | flops 8912384 | bytes 17829888 | tf_op jit(solution)/shard_map/while/body/eval_jaxpr/while/body/eval_jaxpr/reduce_sum | solution.py:58
  320.4 9.3 %fusion.45 = bf16[2,512,128]{2,1,0:T(8,128)(2,1)S(1)} fusion(bf16[2,512,128]{2,1,0:T(8,128)(2,1)S(1)} %get-tuple-element.642, s32[]{:T(128)} %get-tuple-element.641, bf16[8704,128]{1,0:T(8,128)(2,1)} %get-tuple-element.657, f32[512,8704]{1,0:T(8,128)} %get-tuple-element.630, f32[512]{0:T(512)S(1)} %get-tuple-element.631, f32[512]{0:T(512)S(1)} %fusion.44), kind=kOutput, calls=%fused_computation.17.clone.1 | convolution fusion | flops 1149894656 | bytes 20189188 | tf_op jit(solution)/shard_map/while/body/eval_jaxpr/while/body/eval_jaxpr/rk,kd->rd/dot_general | solution.py:59
  330.3 0.6 add_select_fusion.2
  330.9 13.1 %fusion.43 = (f32[512]{0:T(512)S(1)}, f32[512,8704]{1,0:T(8,128)}) fusion(bf16[8704,128]{1,0:T(8,128)(2,1)} %get-tuple-element.656, bf16[2,512,128]{2,1,0:T(8,128)(2,1)S(1)} %get-tuple-element.655, s32[]{:T(128)} %get-tuple-element.641, s32[8704]{0:T(1024)S(1)} %get-tuple-element.625, pred[8704]{0:T(1024)(128)(4,1)S(1)} %get-tuple-element.626, ...), kind=kOutput, calls=%fused_computation.75.clone.1 | convolution fusion | flops 1185414656 | bytes 20290564 | tf_op jit(solution)/shard_map/while/body/eval_jaxpr/while/body/eval_jaxpr/rd,kd->rk/dot_general | solution.py:51
  344.0 8.5 %fusion.44 = f32[512]{0:T(512)S(1)} fusion(f32[512,8704]{1,0:T(8,128)} %get-tuple-element.630, f32[512]{0:T(512)S(1)} %get-tuple-element.631), kind=kLoop, calls=%fused_computation.10.clone.1 | loop fusion | flops 8912384 | bytes 17829888 | tf_op jit(solution)/shard_map/while/body/eval_jaxpr/while/body/eval_jaxpr/reduce_sum | solution.py:58
  352.5 9.3 %fusion.45 = bf16[2,512,128]{2,1,0:T(8,128)(2,1)S(1)} fusion(bf16[2,512,128]{2,1,0:T(8,128)(2,1)S(1)} %get-tuple-element.642, s32[]{:T(128)} %get-tuple-element.641, bf16[8704,128]{1,0:T(8,128)(2,1)} %get-tuple-element.657, f32[512,8704]{1,0:T(8,128)} %get-tuple-element.630, f32[512]{0:T(512)S(1)} %get-tuple-element.631, f32[512]{0:T(512)S(1)} %fusion.44), kind=kOutput, calls=%fused_computation.17.clone.1 | convolution fusion | flops 1149894656 | bytes 20189188 | tf_op jit(solution)/shard_map/while/body/eval_jaxpr/while/body/eval_jaxpr/rk,kd->rd/dot_general | solution.py:59
  361.9 0.8 copy-done.7
  362.7 1.0 copy-done.1
  (59 shorter events, 5.2 us)
Async XLA Ops:
  0.0 5.8 %copy-start = (bf16[2,4096,128]{2,1,0:T(8,128)(2,1)S(1)}, bf16[2,4096,128]{2,1,0:T(8,128)(2,1)}, u32[]{:S(2)}) copy-start(bf16[2,4096,128]{2,1,0:T(8,128)(2,1)} %param.19) | copy-start | bytes 6291460
  7.9 4.0 %copy-start.3 = (bf16[32,256,128]{2,1,0:T(8,128)(2,1)S(1)}, bf16[32,256,128]{2,1,0:T(8,128)(2,1)}, u32[]{:S(2)}) copy-start(bf16[32,256,128]{2,1,0:T(8,128)(2,1)} %gather_fusion.3) | copy-start | bytes 6291460
  16.7 54.5 %all-to-all-start = ((bf16[2,16,256,128]{3,2,0,1:T(8,128)(2,1)}), bf16[2,16,256,128]{3,2,0,1:T(8,128)(2,1)S(1)}, u32[]{:S(2)}, u32[]{:S(2)}) async-start(bf16[2,16,256,128]{3,2,0,1:T(8,128)(2,1)} %copy.18), calls=%async_computation | async-start | bytes 4194304 | tf_op jit(solution)/shard_map/all_to_all | solution.py:111
  71.3 4.5 %copy-start.2 = (bf16[2,16,256,128]{3,2,0,1:T(8,128)(2,1)}, bf16[2,16,256,128]{3,2,0,1:T(8,128)(2,1)S(1)}, u32[]{:S(2)}) copy-start(bf16[2,16,256,128]{3,2,0,1:T(8,128)(2,1)S(1)} %all-to-all-done) | copy-start | bytes 6291460
  71.3 52.3 %all-to-all-start.1 = ((bf16[2,16,256,128]{3,2,0,1:T(8,128)(2,1)}), bf16[2,16,256,128]{3,2,0,1:T(8,128)(2,1)}, u32[]{:S(2)}, u32[]{:S(2)}) async-start(bf16[2,16,256,128]{3,2,0,1:T(8,128)(2,1)} %copy.19), calls=%async_computation.1 | async-start | bytes 4194304 | tf_op jit(solution)/shard_map/all_to_all | solution.py:112
  75.9 51.5 %copy-start.5 = (bf16[2,256,128]{2,1,0:T(8,128)(2,1)S(1)}, bf16[2,256,128]{2,1,0:T(8,128)(2,1)}, u32[]{:S(2)}) copy-start(bf16[2,256,128]{2,1,0:T(8,128)(2,1)} %param.18) | copy-start | bytes 393220
  75.9 55.4 %copy-start.6 = (bf16[2,256,128]{2,1,0:T(8,128)(2,1)S(1)}, bf16[2,256,128]{2,1,0:T(8,128)(2,1)}, u32[]{:S(2)}) copy-start(bf16[2,256,128]{2,1,0:T(8,128)(2,1)} %param.17) | copy-start | bytes 393220
  78.5 79.8 %collective-permute-start = (bf16[2,16,256,128]{3,2,1,0:T(8,128)(2,1)S(1)}, bf16[2,16,256,128]{3,2,1,0:T(8,128)(2,1)}, u32[]{:S(2)}, u32[]{:S(2)}) collective-permute-start(bf16[2,16,256,128]{3,2,1,0:T(8,128)(2,1)S(1)} %bitcast.58), channel_id=1, source_target_pairs={{0,4},{4,0},{8,12},{12,8},{1,5},{5,1},{9,13},{13,9},{2,6},{6,2},{1... | collective-permute-start | bytes 6291464 | tf_op jit(solution)/shard_map/ppermute | solution.py:28
  127.3 73.9 %collective-permute-start.2 = (bf16[2,16,256,128]{3,2,1,0:T(8,128)(2,1)}, bf16[2,16,256,128]{3,2,1,0:T(8,128)(2,1)}, u32[]{:S(2)}, u32[]{:S(2)}) collective-permute-start(bf16[2,16,256,128]{3,2,1,0:T(8,128)(2,1)} %bitcast.60), channel_id=1, source_target_pairs={{0,4},{4,0},{8,12},{12,8},{1,5},{5,1},{9,13},{13,9},{2,6},{6,2},{1... | collective-permute-start | bytes 6291464 | tf_op jit(solution)/shard_map/ppermute | solution.py:28
  127.3 77.5 %collective-permute-start.3 = (bf16[2,256,128]{2,1,0:T(8,128)(2,1)S(1)}, bf16[2,256,128]{2,1,0:T(8,128)(2,1)S(1)}, u32[]{:S(2)}, u32[]{:S(2)}) collective-permute-start(bf16[2,256,128]{2,1,0:T(8,128)(2,1)S(1)} %copy-done.5), channel_id=1, source_target_pairs={{0,4},{4,8},{8,12},{1,5},{5,9},{9,13},{2,6},{6,10},{10,14},{3,7},{... | collective-permute-start | bytes 393224 | tf_op jit(solution)/shard_map/ppermute | solution.py:14
  131.3 83.9 %collective-permute-start.1 = (bf16[2,256,128]{2,1,0:T(8,128)(2,1)S(1)}, bf16[2,256,128]{2,1,0:T(8,128)(2,1)S(1)}, u32[]{:S(2)}, u32[]{:S(2)}) collective-permute-start(bf16[2,256,128]{2,1,0:T(8,128)(2,1)S(1)} %copy-done.6), channel_id=1, source_target_pairs={{0,4},{4,8},{8,12},{1,5},{5,9},{9,13},{2,6},{6,10},{10,14},{3,7},{... | collective-permute-start | bytes 393224 | tf_op jit(solution)/shard_map/ppermute | solution.py:14
  215.2 9.9 %copy-start.4 = (bf16[8,256,128]{2,1,0:T(8,128)(2,1)S(1)}, bf16[8,256,128]{2,1,0:T(8,128)(2,1)}, u32[]{:S(2)}) copy-start(bf16[8,256,128]{2,1,0:T(8,128)(2,1)} %param.16) | copy-start | bytes 1572868
  361.9 0.8 copy-start.7
  361.9 1.8 copy-start.1
where the time goes:
time: 365 us; the launch traced here: 364 us
  waiting for transfers between devices  155 us (42%)
  matrix products  89.4 us (24%)
  other arithmetic  67.8 us (19%)
  local copies, waits for them, and re-layouts  31.2 us (9%)
  starting transfers between devices  19.4 us (5%)
    ppermute x2, waiting for transfers between devices, partner(): return lax.ppermute(value, axis, pairs)  67.3 us
    dot_general x4, matrix products, attend(): jnp.einsum('rd,kd->rk', query_rows, all_keys, preferred_element_type=jnp....  52.3 us
    all_to_all x1, waiting for transfers between devices, shards(): lax.all_to_all(sent_keys, 'ctx', split_axis=1, concat_axis=1, tiled=True)  45.1 us
    all_to_all x1, waiting for transfers between devices, shards(): lax.all_to_all(sent_values, 'ctx', split_axis=1, concat_axis=1, tiled=True)  43.1 us
    dot_general x4, matrix products, attend(): jnp.einsum('rk,kd->rd', weights.astype(jnp.bfloat16), all_values, preferr...  37.1 us
    reduce_sum x4, other arithmetic, attend(): weight_sum = jnp.sum(weights, axis=-1, keepdims=True)  34.2 us
    gather x6, local copies, waits for them, and re-layouts, pick_rows(): return source[indices]  12.5 us
    concatenate x1, other arithmetic, shards(): jnp.concatenate([live_values, prev_values, stretch_values], axis=1)  9.97 us
  transfers between devices with their start and end apart: 6, of which 4 were waited for; matrix products, arithmetic and copies ran while one was open for 6% of the time, Pallas kernels for 0%

commit v1 on v0

--- a/solution.py
+++ b/solution.py
@@ -1,7 +1,12 @@
+import functools
+import math
+
 import jax
 import jax.numpy as jnp
 import numpy as np
 from jax import lax
+from jax.experimental import pallas as pl
+from jax.experimental.pallas import tpu as pltpu
 from jax.sharding import PartitionSpec as P
 
 BLOCK = 512
@@ -158,6 +163,326 @@
     return result.reshape(kv_dev * q_per_kv, tok_dev, head_dim)
 
 
+ROWS = 512
+
+
+def fold(a, m, l, a2, m2, l2):
+    top = jnp.maximum(m, m2)
+    x, y = jnp.exp2(m - top), jnp.exp2(m2 - top)
+    return a * x + a2 * y, top, l * x + l2 * y
+
+
+def line_kernel(
+    n, tok, picks_ref, table_ref, q_ref, sk_ref, sv_ref, ck_ref, cv_ref, out_ref,
+    qbuf, kbuf, vbuf, skbuf, svbuf, acc, mcol, lcol, tx, txs, rxl, rxls, rxr, rxrs,
+    spots, local_sem, q_right, q_left, q_recv, p_send, s_send,
+    pl_recv, sl_recv, pr_recv, sr_recv,
+):
+    me = lax.axis_index("ctx")
+    rows, head_dim = q_ref.shape
+    kv_dev, blocks_dev = ck_ref.shape[:2]
+    chunks = rows // ROWS
+    per_head = chunks // kv_dev
+    per = TOPK // n
+    qblocks = picks_ref.shape[0]
+    scale = head_dim ** (-0.5) * math.log2(math.e)
+    mesh_id = pl.DeviceIdType.MESH
+    has_left, has_right = me > 0, me < n - 1
+    left, right = {"ctx": me - 1}, {"ctx": me + 1}
+
+    def part(c):
+        return pl.ds(pl.multiple_of(c * ROWS, ROWS), ROWS)
+
+    def send_q(src, c, to, sems, own=False):
+        return pltpu.make_async_remote_copy(
+            src_ref=q_ref.at[part(c)] if own else qbuf.at[src, part(c)],
+            dst_ref=qbuf.at[src, part(c)],
+            send_sem=sems.at[src, c], recv_sem=q_recv.at[src, c],
+            device_id=to, device_id_type=mesh_id,
+        )
+
+    def send_p(t, c, to, rx, rxs, sem, ssem):
+        return (
+            pltpu.make_async_remote_copy(
+                src_ref=tx.at[t, part(c)], dst_ref=rx.at[t, part(c)],
+                send_sem=p_send.at[t, c], recv_sem=sem.at[t, c],
+                device_id=to, device_id_type=mesh_id,
+            ),
+            pltpu.make_async_remote_copy(
+                src_ref=txs.at[t, c], dst_ref=rxs.at[t, c],
+                send_sem=s_send.at[t, c], recv_sem=ssem.at[t, c],
+                device_id=to, device_id_type=mesh_id,
+            ),
+        )
+
+    to_right = (right, rxl, rxls, pl_recv, sl_recv)
+    to_left = (left, rxr, rxrs, pr_recv, sr_recv)
+
+    loads = [
+        pltpu.make_async_copy(src, dst, local_sem.at[k])
+        for k, (src, dst) in enumerate((
+            (q_ref, qbuf.at[me]), (sk_ref, skbuf), (sv_ref, svbuf),
+            (ck_ref, kbuf), (cv_ref, vbuf),
+        ))
+    ]
+    for load in loads:
+        load.start()
+
+    barrier = pltpu.get_barrier_semaphore()
+
+    @pl.when(has_left)
+    def _():
+        pl.semaphore_signal(barrier, inc=1, device_id=left, device_id_type=mesh_id)
+
+    @pl.when(has_right)
+    def _():
+        pl.semaphore_signal(barrier, inc=1, device_id=right, device_id_type=mesh_id)
+
+    pl.semaphore_wait(barrier, jnp.where(has_left, 1, 0) + jnp.where(has_right, 1, 0))
+
+    for c in range(chunks):
+        @pl.when(has_right)
+        def _():
+            send_q(me, c, right, q_right, True).start()
+
+        @pl.when(has_left)
+        def _():
+            send_q(me, c, left, q_left, True).start()
+
+    first_head = (lax.axis_index("head") * lax.axis_size("tp") + lax.axis_index("tp")) * kv_dev
+    for j in range(qblocks):
+        for g in range(kv_dev):
+            found = [jnp.int32(0)] * per
+            count = jnp.int32(0)
+            for k in range(TOPK):
+                slot = table_ref[picks_ref[j, first_head + g, k]]
+                spot = slot - me * blocks_dev
+                here = (spot >= 0) & (spot < blocks_dev)
+                for r in range(per):
+                    found[r] = jnp.where(here & (count == r), spot, found[r])
+                count = count + jnp.where(here, 1, 0)
+            for r in range(per):
+                spots[j, g, r] = found[r]
+
+    for load in loads:
+        load.wait()
+
+    def score(t, c, window):
+        g = c // per_head
+        j = t * tok // BLOCK
+        picked = [spots[j, g, r] for r in range(per)]
+        for h in range(ROWS // tok):
+            at = pl.ds(pl.multiple_of(c * ROWS + h * tok, tok), tok)
+            q = qbuf[t, at, :]
+            parts = [
+                lax.dot_general(
+                    q, kbuf[g, spot], (((1,), (1,)), ((), ())),
+                    preferred_element_type=jnp.float32,
+                )
+                for spot in picked
+            ]
+            if window:
+                s = lax.dot_general(
+                    q, skbuf[g], (((1,), (1,)), ((), ())),
+                    preferred_element_type=jnp.float32,
+                )
+                row = lax.broadcasted_iota(jnp.int32, s.shape, 0)
+                col = lax.broadcasted_iota(jnp.int32, s.shape, 1)
+                own = jnp.where(t == me, 1, 0)
+                lead = (row - col) * (2 * own - 1) + own
+                parts.append(jnp.where(lead > 0, s, -jnp.inf))
+            top = functools.reduce(
+                jnp.maximum, [jnp.max(s, axis=1, keepdims=True) for s in parts]
+            ) * scale
+            total = jnp.zeros((tok, head_dim), jnp.float32)
+            norm = jnp.zeros((tok, 1), jnp.float32)
+            for k, s in enumerate(parts):
+                w = jnp.exp2(s * scale - top)
+                norm = norm + jnp.sum(w, axis=1, keepdims=True)
+                v = vbuf[g, picked[k]] if k < per else svbuf[g]
+                total = total + jnp.dot(
+                    w.astype(jnp.bfloat16), v, preferred_element_type=jnp.float32
+                )
+            acc[t, at, :] = total
+            mcol[t, at, :] = top
+            lcol[t, at, :] = norm
+
+    def compute(t, c):
+        near = (t == me) | (t == me + 1)
+
+        @pl.when(near)
+        def _():
+            score(t, c, True)
+
+        @pl.when(jnp.logical_not(near))
+        def _():
+            score(t, c, False)
+
+    eye = (
+        lax.broadcasted_iota(jnp.int32, (128, 128), 0)
+        == lax.broadcasted_iota(jnp.int32, (128, 128), 1)
+    )
+
+    def to_row(col):
+        return jnp.sum(jnp.where(eye, col, 0.0), axis=0, keepdims=True)
+
+    def to_col(row):
+        return jnp.sum(jnp.where(eye, row, 0.0), axis=1, keepdims=True)
+
+    cuts = ROWS // 128
+
+    def fold_in(t, c, rx, rxs):
+        for k in range(cuts):
+            at = pl.ds(pl.multiple_of(c * ROWS + k * 128, 128), 128)
+            a, m, l = fold(
+                acc[t, at, :], mcol[t, at, :], lcol[t, at, :],
+                rx[t, at, :].astype(jnp.float32),
+                to_col(rxs[t, c, k:k + 1, :]), to_col(rxs[t, c, cuts + k:cuts + k + 1, :]),
+            )
+            acc[t, at, :] = a
+            mcol[t, at, :] = m
+            lcol[t, at, :] = l
+
+    def pack(t, c):
+        for k in range(cuts):
+            at = pl.ds(pl.multiple_of(c * ROWS + k * 128, 128), 128)
+            tx[t, at, :] = acc[t, at, :].astype(jnp.bfloat16)
+            txs[t, c, k:k + 1, :] = to_row(mcol[t, at, :])
+            txs[t, c, cuts + k:cuts + k + 1, :] = to_row(lcol[t, at, :])
+
+    def hand_on(t, c, upstream, way):
+        @pl.when(upstream)
+        def _():
+            for copy in send_p(t, c, *way):
+                copy.wait_recv()
+            fold_in(t, c, way[1], way[2])
+
+        pack(t, c)
+        for copy in send_p(t, c, *way):
+            copy.start()
+
+    def each(body):
+        lax.fori_loop(0, chunks, lambda c, z: (body(c), z)[1], 0)
+
+    each(lambda c: compute(me, c))
+
+    for b in range(1, n):
+        def arrive(c, b=b):
+            @pl.when(me >= b)
+            def _():
+                send_q(me - b, c, right, q_right).wait_recv()
+
+                @pl.when(has_right)
+                def _():
+                    send_q(me - b, c, right, q_right).start()
+
+            @pl.when(me + b < n)
+            def _():
+                send_q(me + b, c, left, q_left).wait_recv()
+
+                @pl.when(has_left)
+                def _():
+                    send_q(me + b, c, left, q_left).start()
+
+            @pl.when(me + b < n)
+            def _():
+                compute(me + b, c)
+
+            @pl.when(me >= b)
+            def _():
+                compute(me - b, c)
+
+        def depart(c, b=b):
+            @pl.when((b > me) & has_right)
+            def _():
+                hand_on(b, c, has_left, to_right)
+
+            @pl.when((b > n - 1 - me) & has_left)
+            def _():
+                hand_on(n - 1 - b, c, has_right, to_left)
+
+        each(arrive)
+        each(depart)
+
+    def finish(c):
+        @pl.when(has_left)
+        def _():
+            for copy in send_p(me, c, *to_right):
+                copy.wait_recv()
+            fold_in(me, c, rxl, rxls)
+
+        @pl.when(has_right)
+        def _():
+            for copy in send_p(me, c, *to_left):
+                copy.wait_recv()
+            fold_in(me, c, rxr, rxrs)
+
+        out_ref[part(c), :] = (acc[me, part(c), :] / lcol[me, part(c), :]).astype(out_ref.dtype)
+
+    each(finish)
+
+    def drain(c):
+        for s in range(n):
+            @pl.when((s <= me) & has_right)
+            def _():
+                send_q(s, c, right, q_right).wait_send()
+
+            @pl.when((s >= me) & has_left)
+            def _():
+                send_q(s, c, left, q_left).wait_send()
+
+            @pl.when(s > me)
+            def _():
+                for copy in send_p(s, c, *to_right):
+                    copy.wait_send()
+
+            @pl.when(s < me)
+            def _():
+                for copy in send_p(s, c, *to_left):
+                    copy.wait_send()
+
+    each(drain)
+
+
+def line_shards(
+    queries, stretch_keys, stretch_values, cache_keys, cache_values, block_picks, block_table
+):
+    n = lax.axis_size("ctx")
+    kv_dev, tok, head_dim = stretch_keys.shape
+    rows = queries.shape[0] * tok
+    chunks = rows // ROWS
+    by_block = (kv_dev, cache_keys.shape[1] // BLOCK, BLOCK, head_dim)
+    any_space = pl.BlockSpec(memory_space=pl.ANY)
+    smem = pl.BlockSpec(memory_space=pltpu.SMEM)
+    bf16, f32 = jnp.bfloat16, jnp.float32
+    stats = pltpu.VMEM((n, chunks, 8, 128), f32)
+    rows_bf16 = pltpu.VMEM((n, rows, head_dim), bf16)
+    column = pltpu.VMEM((n, rows, 1), f32)
+    sems = pltpu.SemaphoreType.DMA((n, chunks))
+    result = pl.pallas_call(
+        functools.partial(line_kernel, n, tok),
+        out_shape=jax.ShapeDtypeStruct((rows, head_dim), bf16),
+        in_specs=[smem, smem] + [any_space] * 5,
+        out_specs=pl.BlockSpec(memory_space=pltpu.VMEM),
+        scratch_shapes=[
+            rows_bf16,
+            pltpu.VMEM(by_block, bf16), pltpu.VMEM(by_block, bf16),
+            pltpu.VMEM(stretch_keys.shape, bf16), pltpu.VMEM(stretch_values.shape, bf16),
+            pltpu.VMEM((n, rows, head_dim), f32), column, column,
+            rows_bf16, stats, rows_bf16, stats, rows_bf16, stats,
+            pltpu.SMEM((block_picks.shape[0], kv_dev, TOPK // n), jnp.int32),
+            pltpu.SemaphoreType.DMA((5,)),
+        ] + [sems] * 9,
+        compiler_params=pltpu.CompilerParams(
+            collective_id=0, has_side_effects=True, vmem_limit_bytes=56 * 2**20
+        ),
+    )(
+        block_picks, block_table, queries.reshape(rows, head_dim),
+        stretch_keys, stretch_values, cache_keys.reshape(by_block), cache_values.reshape(by_block),
+    )
+    return result.reshape(queries.shape)
+
+
 def solution(mesh):
     placed = (
         P(("head", "tp"), ("groups", "ctx"), None),
@@ -168,8 +493,9 @@
         P("groups", None, None),
         P("groups"),
     )
+    few = TOPK % mesh.shape["ctx"] == 0
     return jax.shard_map(
-        shards,
+        line_shards if few else shards,
         mesh=mesh,
         in_specs=placed,
         out_specs=P(("head", "tp"), ("groups", "ctx"), None),

time: 365 us -> 101 us (0.28)
  waiting for transfers between devices: 155 us -> 0 us
  Pallas kernels: 0 us -> 99.1 us
  matrix products: 89.4 us -> 0 us
  other arithmetic: 67.8 us -> 0 us
  local copies, waits for them, and re-layouts: 31.2 us -> 1.87 us
  starting transfers between devices: 19.4 us -> 0 us
    pallas_call x0 -> x1, Pallas kernels: none -> 99.1 us  [line_shards(): pl.pallas_call(functools.partial(line_kernel, n, tok), out_shape=jax.Shap...]
    dot_general x8 -> x0, matrix products: 89.4 us -> none  [the longest x4 52.3 us: attend(): jnp.einsum('rd,kd->rk', query_rows, all_keys, preferred_element_type=jnp....]
    all_to_all x2 -> x0, waiting for transfers between devices: 88.2 us -> none  [the longest x1 45.1 us: shards(): lax.all_to_all(sent_keys, 'ctx', split_axis=1, concat_axis=1, tiled=True)]
    ppermute x4 -> x0, waiting for transfers between devices: 67.3 us -> none  [the longest x2 67.3 us: partner(): return lax.ppermute(value, axis, pairs)]
    reduce_sum x8 -> x0, other arithmetic: 36.4 us -> none  [the longest x4 34.2 us: attend(): weight_sum = jnp.sum(weights, axis=-1, keepdims=True)]
    concatenate x4 -> x0, other arithmetic: 20.7 us -> none  [the longest x1 9.97 us: shards(): jnp.concatenate([live_values, prev_values, stretch_values], axis=1)]
    gather x9 -> x0, local copies, waits for them, and re-layouts: 14.2 us -> none  [the longest x6 12.5 us: pick_rows(): return source[indices]]
    all_to_all x2 -> x0, starting transfers between devices: 10.8 us -> none  [the longest x1 6.33 us: shards(): lax.all_to_all(sent_keys, 'ctx', split_axis=1, concat_axis=1, tiled=True)]
  transfers between devices with their start and end apart: 6 -> 0, of which waited for: 4 -> 0; matrix products, arithmetic and copies ran while one was open for 6% -> 0% of each run, Pallas kernels for 0% -> 0%
where the time goes in v1:
time: 101 us
  Pallas kernels  99.1 us (98%)
  local copies, waits for them, and re-layouts  1.87 us (2%)
    pallas_call x1, Pallas kernels, line_shards(): pl.pallas_call(functools.partial(line_kernel, n, tok), out_shape=jax.Shap...  99.1 us

profile of v1, /device:TPU:0, one launch (start us, length us, event | category | flops | bytes accessed | tf_op | source)
XLA Modules:
  0.0 101.0 jit_solution(10729576987717907793)
XLA Ops:
  0.0 99.1 %shard_map.73 = bf16[2048,128]{1,0:T(8,128)(2,1)} custom-call(s32[2,8,16]{2,1,0:T(8,128)} %picks_ref.1, s32[32]{0:T(128)} %table_ref.1, bf16[2048,128]{1,0:T(8,128)(2,1)} %bitcast.7, bf16[2,256,128]{2,1,0:T(8,128)(2,1)} %sk_ref.1, bf16[2,256,128]{2,1,0:T(8,128)(2,1)} %sv_ref.1, bf16[2,8,512,128]{3,2,1,0:T(8,128)(2,1)} %bitcast.4, ...), custom_call_target="tpu_custom_call" | custom-call | tf_op jit(solution)/shard_map/pallas_call | solution.py:462
  99.1 1.9 %copy.9 = bf16[8,256,128]{2,1,0:T(8,128)(2,1)} copy(bf16[8,256,128]{2,1,0:T(8,128)(2,1)} %bitcast.6) | data formatting | bytes 1048576

commit v2 on v1

--- a/solution.py
+++ b/solution.py
@@ -267,6 +267,9 @@
     for load in loads:
         load.wait()
 
+    def lanes(x):
+        return [x[:, k:k + 128] for k in range(0, x.shape[1], 128)]
+
     def score(t, c, window):
         g = c // per_head
         j = t * tok // BLOCK
@@ -291,21 +294,24 @@
                 own = jnp.where(t == me, 1, 0)
                 lead = (row - col) * (2 * own - 1) + own
                 parts.append(jnp.where(lead > 0, s, -jnp.inf))
-            top = functools.reduce(
-                jnp.maximum, [jnp.max(s, axis=1, keepdims=True) for s in parts]
+            top = jnp.max(
+                functools.reduce(jnp.maximum, [x for s in parts for x in lanes(s)]),
+                axis=1, keepdims=True,
             ) * scale
             total = jnp.zeros((tok, head_dim), jnp.float32)
-            norm = jnp.zeros((tok, 1), jnp.float32)
+            sums = []
             for k, s in enumerate(parts):
                 w = jnp.exp2(s * scale - top)
-                norm = norm + jnp.sum(w, axis=1, keepdims=True)
+                sums.append(functools.reduce(jnp.add, lanes(w)))
                 v = vbuf[g, picked[k]] if k < per else svbuf[g]
                 total = total + jnp.dot(
                     w.astype(jnp.bfloat16), v, preferred_element_type=jnp.float32
                 )
             acc[t, at, :] = total
             mcol[t, at, :] = top
-            lcol[t, at, :] = norm
+            lcol[t, at, :] = jnp.sum(
+                functools.reduce(jnp.add, sums), axis=1, keepdims=True
+            )
 
     def compute(t, c):
         near = (t == me) | (t == me + 1)
@@ -331,43 +337,46 @@
 
     cuts = ROWS // 128
 
-    def fold_in(t, c, rx, rxs):
-        for k in range(cuts):
-            at = pl.ds(pl.multiple_of(c * ROWS + k * 128, 128), 128)
-            a, m, l = fold(
-                acc[t, at, :], mcol[t, at, :], lcol[t, at, :],
-                rx[t, at, :].astype(jnp.float32),
-                to_col(rxs[t, c, k:k + 1, :]), to_col(rxs[t, c, cuts + k:cuts + k + 1, :]),
-            )
-            acc[t, at, :] = a
-            mcol[t, at, :] = m
-            lcol[t, at, :] = l
-
-    def pack(t, c):
-        for k in range(cuts):
-            at = pl.ds(pl.multiple_of(c * ROWS + k * 128, 128), 128)
-            tx[t, at, :] = acc[t, at, :].astype(jnp.bfloat16)
-            txs[t, c, k:k + 1, :] = to_row(mcol[t, at, :])
-            txs[t, c, cuts + k:cuts + k + 1, :] = to_row(lcol[t, at, :])
-
-    def hand_on(t, c, upstream, way):
-        @pl.when(upstream)
-        def _():
+    def at_cut(c, k):
+        return pl.ds(pl.multiple_of(c * ROWS + k * 128, 128), 128)
+
+    def own_part(t, c, k):
+        at = at_cut(c, k)
+        return acc[t, at, :], mcol[t, at, :], lcol[t, at, :]
+
+    def merged(state, t, c, k, rx, rxs):
+        return fold(
+            *state, rx[t, at_cut(c, k), :].astype(jnp.int32).astype(jnp.float32),
+            to_col(rxs[t, c, k:k + 1, :]), to_col(rxs[t, c, cuts + k:cuts + k + 1, :]),
+        )
+
+    def pack(state, t, c, k):
+        a, m, l = state
+        peak = jnp.maximum(jnp.max(jnp.abs(a), axis=1, keepdims=True), 1e-25)
+        per_unit = 32767.0 / peak
+        tx[t, at_cut(c, k), :] = jnp.round(a * per_unit).astype(jnp.int32).astype(jnp.int16)
+        txs[t, c, k:k + 1, :] = to_row(m - jnp.log(per_unit) * math.log2(math.e))
+        txs[t, c, cuts + k:cuts + k + 1, :] = to_row(l * per_unit)
+
+    def hand_on(t, c, way, relay):
+        if relay:
             for copy in send_p(t, c, *way):
                 copy.wait_recv()
-            fold_in(t, c, way[1], way[2])
-
-        pack(t, c)
+        for k in range(cuts):
+            state = own_part(t, c, k)
+            if relay:
+                state = merged(state, t, c, k, way[1], way[2])
+            pack(state, t, c, k)
         for copy in send_p(t, c, *way):
             copy.start()
 
-    def each(body):
-        lax.fori_loop(0, chunks, lambda c, z: (body(c), z)[1], 0)
-
-    each(lambda c: compute(me, c))
+    def each(body, count=chunks):
+        lax.fori_loop(0, count, lambda c, z: (body(c), z)[1], 0)
+
+    inner = has_left & has_right
 
     for b in range(1, n):
-        def arrive(c, b=b):
+        def step(c, b=b):
             @pl.when(me >= b)
             def _():
                 send_q(me - b, c, right, q_right).wait_recv()
@@ -392,32 +401,67 @@
             def _():
                 compute(me - b, c)
 
-        def depart(c, b=b):
-            @pl.when((b > me) & has_right)
-            def _():
-                hand_on(b, c, has_left, to_right)
-
-            @pl.when((b > n - 1 - me) & has_left)
-            def _():
-                hand_on(n - 1 - b, c, has_right, to_left)
-
-        each(arrive)
-        each(depart)
+            @pl.when(me == 0)
+            def _():
+                hand_on(b, c, to_right, False)
+
+            @pl.when(me == n - 1)
+            def _():
+                hand_on(n - 1 - b, c, to_left, False)
+
+            if b < n - 1:
+                @pl.when(has_left & (me < b))
+                def _():
+                    hand_on(b, c, to_right, True)
+
+                @pl.when(has_right & (me > n - 1 - b))
+                def _():
+                    hand_on(n - 1 - b, c, to_left, True)
+
+        each(step)
+
+    def last(k):
+        c_right, c_left = k - (me - 1), k - (n - 2 - me)
+
+        @pl.when(inner & (c_right >= 0) & (c_right < chunks))
+        def _():
+            hand_on(n - 1, c_right, to_right, True)
+
+        @pl.when(inner & (c_left >= 0) & (c_left < chunks))
+        def _():
+            hand_on(0, c_left, to_left, True)
+
+        @pl.when(k < chunks)
+        def _():
+            score(me, k, True)
+
+    each(last, chunks + max(n - 3, 0))
 
     def finish(c):
         @pl.when(has_left)
         def _():
             for copy in send_p(me, c, *to_right):
                 copy.wait_recv()
-            fold_in(me, c, rxl, rxls)
 
         @pl.when(has_right)
         def _():
             for copy in send_p(me, c, *to_left):
                 copy.wait_recv()
-            fold_in(me, c, rxr, rxrs)
-
-        out_ref[part(c), :] = (acc[me, part(c), :] / lcol[me, part(c), :]).astype(out_ref.dtype)
+
+        def close(from_left, from_right):
+            for k in range(cuts):
+                state = own_part(me, c, k)
+                if from_left:
+                    state = merged(state, me, c, k, rxl, rxls)
+                if from_right:
+                    state = merged(state, me, c, k, rxr, rxrs)
+                out_ref[at_cut(c, k), :] = (state[0] / state[2]).astype(out_ref.dtype)
+
+        for from_left in (False, True):
+            for from_right in (False, True):
+                @pl.when((has_left == from_left) & (has_right == from_right))
+                def _():
+                    close(from_left, from_right)
 
     each(finish)
 
@@ -457,6 +501,7 @@
     bf16, f32 = jnp.bfloat16, jnp.float32
     stats = pltpu.VMEM((n, chunks, 8, 128), f32)
     rows_bf16 = pltpu.VMEM((n, rows, head_dim), bf16)
+    rows_int = pltpu.VMEM((n, rows, head_dim), jnp.int16)
     column = pltpu.VMEM((n, rows, 1), f32)
     sems = pltpu.SemaphoreType.DMA((n, chunks))
     result = pl.pallas_call(
@@ -469,7 +514,7 @@
             pltpu.VMEM(by_block, bf16), pltpu.VMEM(by_block, bf16),
             pltpu.VMEM(stretch_keys.shape, bf16), pltpu.VMEM(stretch_values.shape, bf16),
             pltpu.VMEM((n, rows, head_dim), f32), column, column,
-            rows_bf16, stats, rows_bf16, stats, rows_bf16, stats,
+            rows_int, stats, rows_int, stats, rows_int, stats,
             pltpu.SMEM((block_picks.shape[0], kv_dev, TOPK // n), jnp.int32),
             pltpu.SemaphoreType.DMA((5,)),
         ] + [sems] * 9,

time: 101 us -> 74.4 us (0.74)
  Pallas kernels: 99.1 us -> 72.4 us
    pallas_call x1, Pallas kernels: 99.1 us -> 72.4 us  [line_shards(): pl.pallas_call(functools.partial(line_kernel, n, tok), out_shape=jax.Shap...]
where the time goes in v2:
time: 74.4 us; the launch traced here: 74.2 us
  Pallas kernels  72.4 us (97%)
  local copies, waits for them, and re-layouts  1.87 us (3%)
    pallas_call x1, Pallas kernels, line_shards(): pl.pallas_call(functools.partial(line_kernel, n, tok), out_shape=jax.Shap...  72.4 us
    unnamed x1, local copies, waits for them, and re-layouts  1.87 us

profile of v2, /device:TPU:0, one launch (start us, length us, event | category | flops | bytes accessed | tf_op | source)
XLA Modules:
  0.0 74.2 jit_solution(15177541691754376489)
XLA Ops:
  0.0 72.4 %shard_map.73 = bf16[2048,128]{1,0:T(8,128)(2,1)} custom-call(s32[2,8,16]{2,1,0:T(8,128)} %picks_ref.1, s32[32]{0:T(128)} %table_ref.1, bf16[2048,128]{1,0:T(8,128)(2,1)} %bitcast.7, bf16[2,256,128]{2,1,0:T(8,128)(2,1)} %sk_ref.1, bf16[2,256,128]{2,1,0:T(8,128)(2,1)} %sv_ref.1, bf16[2,8,512,128]{3,2,1,0:T(8,128)(2,1)} %bitcast.4, ...), custom_call_target="tpu_custom_call" | custom-call | tf_op jit(solution)/shard_map/pallas_call | solution.py:507
  72.4 1.9 %copy.9 = bf16[8,256,128]{2,1,0:T(8,128)(2,1)} copy(bf16[8,256,128]{2,1,0:T(8,128)(2,1)} %bitcast.6) | data formatting | bytes 1048576

commit v3 on v2

--- a/solution.py
+++ b/solution.py
@@ -274,44 +274,47 @@
         g = c // per_head
         j = t * tok // BLOCK
         picked = [spots[j, g, r] for r in range(per)]
-        for h in range(ROWS // tok):
-            at = pl.ds(pl.multiple_of(c * ROWS + h * tok, tok), tok)
-            q = qbuf[t, at, :]
-            parts = [
-                lax.dot_general(
-                    q, kbuf[g, spot], (((1,), (1,)), ((), ())),
-                    preferred_element_type=jnp.float32,
-                )
-                for spot in picked
-            ]
-            if window:
-                s = lax.dot_general(
-                    q, skbuf[g], (((1,), (1,)), ((), ())),
-                    preferred_element_type=jnp.float32,
-                )
-                row = lax.broadcasted_iota(jnp.int32, s.shape, 0)
-                col = lax.broadcasted_iota(jnp.int32, s.shape, 1)
-                own = jnp.where(t == me, 1, 0)
-                lead = (row - col) * (2 * own - 1) + own
-                parts.append(jnp.where(lead > 0, s, -jnp.inf))
+        heads = ROWS // tok
+        at = [pl.ds(pl.multiple_of(c * ROWS + h * tok, tok), tok) for h in range(heads)]
+        queries = [qbuf[t, rows_at, :] for rows_at in at]
+        pieces = per + 1 if window else per
+
+        def scores(h, k):
+            s = lax.dot_general(
+                queries[h], kbuf[g, picked[k]] if k < per else skbuf[g],
+                (((1,), (1,)), ((), ())), preferred_element_type=jnp.float32,
+            )
+            if k < per:
+                return s
+            row = lax.broadcasted_iota(jnp.int32, s.shape, 0)
+            col = lax.broadcasted_iota(jnp.int32, s.shape, 1)
+            own = jnp.where(t == me, 1, 0)
+            lead = (row - col) * (2 * own - 1) + own
+            return jnp.where(lead > 0, s, -jnp.inf)
+
+        parts = [scores(0, k) for k in range(pieces)]
+        for h in range(heads):
             top = jnp.max(
                 functools.reduce(jnp.maximum, [x for s in parts for x in lanes(s)]),
                 axis=1, keepdims=True,
             ) * scale
             total = jnp.zeros((tok, head_dim), jnp.float32)
-            sums = []
+            sums, later = [], []
             for k, s in enumerate(parts):
+                if h + 1 < heads:
+                    later.append(scores(h + 1, k))
                 w = jnp.exp2(s * scale - top)
                 sums.append(functools.reduce(jnp.add, lanes(w)))
                 v = vbuf[g, picked[k]] if k < per else svbuf[g]
                 total = total + jnp.dot(
                     w.astype(jnp.bfloat16), v, preferred_element_type=jnp.float32
                 )
-            acc[t, at, :] = total
-            mcol[t, at, :] = top
-            lcol[t, at, :] = jnp.sum(
+            acc[t, at[h], :] = total
+            mcol[t, at[h], :] = top
+            lcol[t, at[h], :] = jnp.sum(
                 functools.reduce(jnp.add, sums), axis=1, keepdims=True
             )
+            parts = later
 
     def compute(t, c):
         near = (t == me) | (t == me + 1)

time: 74.4 us -> 73.9 us (level)
  no operation moved by 1% of the time
where the time goes in v3:
time: 73.9 us; the launch traced here: 73.7 us
  Pallas kernels  71.8 us (97%)
  local copies, waits for them, and re-layouts  1.87 us (3%)
    pallas_call x1, Pallas kernels, line_shards(): pl.pallas_call(functools.partial(line_kernel, n, tok), out_shape=jax.Shap...  71.8 us
    unnamed x1, local copies, waits for them, and re-layouts  1.87 us

profile of v3, /device:TPU:0, one launch (start us, length us, event | category | flops | bytes accessed | tf_op | source)
XLA Modules:
  0.0 73.7 jit_solution(7926059395612464848)
XLA Ops:
  0.0 71.8 %shard_map.73 = bf16[2048,128]{1,0:T(8,128)(2,1)} custom-call(s32[2,8,16]{2,1,0:T(8,128)} %picks_ref.1, s32[32]{0:T(128)} %table_ref.1, bf16[2048,128]{1,0:T(8,128)(2,1)} %bitcast.7, bf16[2,256,128]{2,1,0:T(8,128)(2,1)} %sk_ref.1, bf16[2,256,128]{2,1,0:T(8,128)(2,1)} %sv_ref.1, bf16[2,8,512,128]{3,2,1,0:T(8,128)(2,1)} %bitcast.4, ...), custom_call_target="tpu_custom_call" | custom-call | tf_op jit(solution)/shard_map/pallas_call | solution.py:510
  71.8 1.9 %copy.9 = bf16[8,256,128]{2,1,0:T(8,128)(2,1)} copy(bf16[8,256,128]{2,1,0:T(8,128)(2,1)} %bitcast.6) | data formatting | bytes 1048576

commit v4 on v3

--- a/solution.py
+++ b/solution.py
@@ -182,7 +182,9 @@
     rows, head_dim = q_ref.shape
     kv_dev, blocks_dev = ck_ref.shape[:2]
     chunks = rows // ROWS
-    per_head = chunks // kv_dev
+    head_rows = rows // kv_dev
+    heads = ROWS // tok
+    early = heads // 2
     per = TOPK // n
     qblocks = picks_ref.shape[0]
     scale = head_dim ** (-0.5) * math.log2(math.e)
@@ -270,12 +272,11 @@
     def lanes(x):
         return [x[:, k:k + 128] for k in range(0, x.shape[1], 128)]
 
-    def score(t, c, window):
-        g = c // per_head
+    def score(t, start, heads, window):
+        g = start // head_rows
         j = t * tok // BLOCK
         picked = [spots[j, g, r] for r in range(per)]
-        heads = ROWS // tok
-        at = [pl.ds(pl.multiple_of(c * ROWS + h * tok, tok), tok) for h in range(heads)]
+        at = [pl.ds(pl.multiple_of(start + h * tok, tok), tok) for h in range(heads)]
         queries = [qbuf[t, rows_at, :] for rows_at in at]
         pieces = per + 1 if window else per
 
@@ -321,11 +322,11 @@
 
         @pl.when(near)
         def _():
-            score(t, c, True)
+            score(t, c * ROWS, heads, True)
 
         @pl.when(jnp.logical_not(near))
         def _():
-            score(t, c, False)
+            score(t, c * ROWS, heads, False)
 
     eye = (
         lax.broadcasted_iota(jnp.int32, (128, 128), 0)
@@ -378,8 +379,13 @@
 
     inner = has_left & has_right
 
+    def own_head(u):
+        score(me, u * tok, 1, True)
+
+    each(own_head, early * chunks)
+
     for b in range(1, n):
-        def step(c, b=b):
+        def receive(c, b=b):
             @pl.when(me >= b)
             def _():
                 send_q(me - b, c, right, q_right).wait_recv()
@@ -395,6 +401,12 @@
                 @pl.when(has_left)
                 def _():
                     send_q(me + b, c, left, q_left).start()
+
+        def step(c, b=b, receive=receive):
+            if b == 1:
+                receive(c)
+            else:
+                pl.when(jnp.logical_not(inner))(lambda: receive(c))
 
             @pl.when(me + b < n)
             def _():
@@ -421,6 +433,8 @@
                 def _():
                     hand_on(n - 1 - b, c, to_left, True)
 
+        if b > 1:
+            pl.when(inner)(lambda: each(receive))
         each(step)
 
     def last(k):
@@ -436,7 +450,8 @@
 
         @pl.when(k < chunks)
         def _():
-            score(me, k, True)
+            for h in range(early, heads):
+                own_head(early * chunks + k * (heads - early) + h - early)
 
     each(last, chunks + max(n - 3, 0))
 

time: 73.9 us -> 72.8 us (0.985)
  Pallas kernels: 71.8 us -> 70.7 us
    pallas_call x1, Pallas kernels: 71.8 us -> 70.7 us  [line_shards(): pl.pallas_call(functools.partial(line_kernel, n, tok), out_shape=jax.Shap...]
where the time goes in v4:
time: 72.8 us; the launch traced here: 72.6 us
  Pallas kernels  70.7 us (97%)
  local copies, waits for them, and re-layouts  1.87 us (3%)
    pallas_call x1, Pallas kernels, line_shards(): pl.pallas_call(functools.partial(line_kernel, n, tok), out_shape=jax.Shap...  70.7 us
    unnamed x1, local copies, waits for them, and re-layouts  1.87 us

profile of v4, /device:TPU:0, one launch (start us, length us, event | category | flops | bytes accessed | tf_op | source)
XLA Modules:
  0.0 72.6 jit_solution(16711692595180736567)
XLA Ops:
  0.0 70.7 %shard_map.73 = bf16[2048,128]{1,0:T(8,128)(2,1)} custom-call(s32[2,8,16]{2,1,0:T(8,128)} %picks_ref.1, s32[32]{0:T(128)} %table_ref.1, bf16[2048,128]{1,0:T(8,128)(2,1)} %bitcast.7, bf16[2,256,128]{2,1,0:T(8,128)(2,1)} %sk_ref.1, bf16[2,256,128]{2,1,0:T(8,128)(2,1)} %sv_ref.1, bf16[2,8,512,128]{3,2,1,0:T(8,128)(2,1)} %bitcast.4, ...), custom_call_target="tpu_custom_call" | custom-call | tf_op jit(solution)/shard_map/pallas_call | solution.py:525
  70.8 1.9 %copy.9 = bf16[8,256,128]{2,1,0:T(8,128)(2,1)} copy(bf16[8,256,128]{2,1,0:T(8,128)(2,1)} %bitcast.6) | data formatting | bytes 1048576

commit v5 on v4

--- a/solution.py
+++ b/solution.py
@@ -163,7 +163,7 @@
     return result.reshape(kv_dev * q_per_kv, tok_dev, head_dim)
 
 
-ROWS = 512
+ROWS = 256
 
 
 def fold(a, m, l, a2, m2, l2):
@@ -184,7 +184,8 @@
     chunks = rows // ROWS
     head_rows = rows // kv_dev
     heads = ROWS // tok
-    early = heads // 2
+    own_heads = rows // tok
+    early = own_heads // 2
     per = TOPK // n
     qblocks = picks_ref.shape[0]
     scale = head_dim ** (-0.5) * math.log2(math.e)
@@ -382,7 +383,7 @@
     def own_head(u):
         score(me, u * tok, 1, True)
 
-    each(own_head, early * chunks)
+    each(own_head, early)
 
     for b in range(1, n):
         def receive(c, b=b):
@@ -448,12 +449,11 @@
         def _():
             hand_on(0, c_left, to_left, True)
 
-        @pl.when(k < chunks)
-        def _():
-            for h in range(early, heads):
-                own_head(early * chunks + k * (heads - early) + h - early)
-
-    each(last, chunks + max(n - 3, 0))
+        @pl.when(k < own_heads - early)
+        def _():
+            own_head(early + k)
+
+    each(last, max(chunks + max(n - 3, 0), own_heads - early))
 
     def finish(c):
         @pl.when(has_left)
@@ -517,7 +517,7 @@
     any_space = pl.BlockSpec(memory_space=pl.ANY)
     smem = pl.BlockSpec(memory_space=pltpu.SMEM)
     bf16, f32 = jnp.bfloat16, jnp.float32
-    stats = pltpu.VMEM((n, chunks, 8, 128), f32)
+    stats = pltpu.VMEM((n, chunks, 2 * ROWS // 128, 128), f32)
     rows_bf16 = pltpu.VMEM((n, rows, head_dim), bf16)
     rows_int = pltpu.VMEM((n, rows, head_dim), jnp.int16)
     column = pltpu.VMEM((n, rows, 1), f32)

time: 72.8 us -> 85.7 us (1.18)
  Pallas kernels: 70.7 us -> 83.6 us
    pallas_call x1, Pallas kernels: 70.7 us -> 83.6 us  [line_shards(): pl.pallas_call(functools.partial(line_kernel, n, tok), out_shape=jax.Shap...]
where the time goes in v5:
time: 85.7 us; the launch traced here: 85.4 us
  Pallas kernels  83.6 us (98%)
  local copies, waits for them, and re-layouts  1.87 us (2%)
    pallas_call x1, Pallas kernels, line_shards(): pl.pallas_call(functools.partial(line_kernel, n, tok), out_shape=jax.Shap...  83.6 us
    unnamed x1, local copies, waits for them, and re-layouts  1.87 us

profile of v5, /device:TPU:0, one launch (start us, length us, event | category | flops | bytes accessed | tf_op | source)
XLA Modules:
  0.0 85.4 jit_solution(5254120937629453235)
XLA Ops:
  0.0 83.6 %shard_map.73 = bf16[2048,128]{1,0:T(8,128)(2,1)} custom-call(s32[2,8,16]{2,1,0:T(8,128)} %picks_ref.1, s32[32]{0:T(128)} %table_ref.1, bf16[2048,128]{1,0:T(8,128)(2,1)} %bitcast.7, bf16[2,256,128]{2,1,0:T(8,128)(2,1)} %sk_ref.1, bf16[2,256,128]{2,1,0:T(8,128)(2,1)} %sv_ref.1, bf16[2,8,512,128]{3,2,1,0:T(8,128)(2,1)} %bitcast.4, ...), custom_call_target="tpu_custom_call" | custom-call | tf_op jit(solution)/shard_map/pallas_call | solution.py:525
  83.6 1.9 %copy.9 = bf16[8,256,128]{2,1,0:T(8,128)(2,1)} copy(bf16[8,256,128]{2,1,0:T(8,128)(2,1)} %bitcast.6) | data formatting | bytes 1048576
